TPU v7x, 256 devices: a whole 4x4x8 slice. The times are simulated.
256 devices in a mesh: slab: 4 (over x), tile: 64 (over z, y, core).
Axes of the slice: x: 4, y: 4, z: 8, core: 2. Of those that a mesh axis runs over, the one named last changes fastest.
Arguments:
- distributions: float32 [7, 128, 256, 256], P(None, 'slab', 'tile'), may hold values from 0 to 0.3
- gate_states: float32 [3, 128, 256, 256], P(None, 'slab', 'tile'), may hold values from 0 to 1
- history: float32 [32, 128, 256, 256], P(None, 'slab', 'tile')
- tissue: int32 [128, 256, 256], P('slab', 'tile'), may hold values from 0 to 3, as said below
- stim_site: int32 [128, 256, 256], P('slab', 'tile'), may hold values from 0 to 8, as said below
- stim_amp: float32 [8], replicated, may hold values from 1 to 10
- record_column: int32 [2], replicated, may hold values from 0 to 31, as said below
Outputs:
- next_distributions: float32 [7, 128, 256, 256], P(None, 'slab', 'tile')
- next_gates: float32 [3, 128, 256, 256], P(None, 'slab', 'tile')
- pod_basis: float32 [32, 128, 256, 256], P(None, 'slab', 'tile')
- upper_factor: float32 [32, 32], replicated
Inputs may be any that keep to these rules, and one draw needn't show every extreme that they name: `tissue`: 0 outside the heart or in a gap; 1 endocardial, 2 midmyocardial, 3 epicardial cells. `stim_site`: 0 means no stimulus; k > 0 drives the voxel with stim_amp[k - 1]. `record_column`: distinct column indices; one of them is the last column.
All inputs are finite; a program needn't handle non-finite values.
Results may differ from a plain program's by a relative error of at most 0.0003.
Values sent between devices are 32-bit elements; how exact they have to be, the bound alone decides.
A program may use at most 128 MiB of HBM per device.

v0:
```python
import functools
import math

import jax
import jax.numpy as jnp
from jax import lax
from jax.experimental import pallas as pl
from jax.experimental.pallas import tpu as pltpu
from jax.sharding import PartitionSpec as P

MESH = pl.DeviceIdType.MESH
DT = 0.1
DEAD = -1e30
LIMIT = -1e29
F32 = jnp.float32
BF16 = jnp.bfloat16
NT = (((1,), (1,)), ((), ()))
GROUP = 16


def split_rows(a, shape):
    lead = a.shape[:-2]
    a = jnp.swapaxes(a.reshape(lead + (4, 2, 128)), -3, -2)
    return a.reshape(shape)


def join_rows(a, shape):
    lead = shape[:-2]
    a = jnp.swapaxes(a.reshape(lead + (2, 4, 128)), -3, -2)
    return a.reshape(shape)


def typed(tissue):
    endo = tissue == 1
    mid = tissue == 2

    def pick(a, b, c):
        if a == b == c:
            return a
        if b == c:
            return jnp.where(endo, F32(a), F32(c))
        if a == c:
            return jnp.where(mid, F32(b), F32(c))
        if a == b:
            return jnp.where(tissue == 1, F32(a), jnp.where(mid, F32(a), F32(c)))
        return jnp.where(endo, F32(a), jnp.where(mid, F32(b), F32(c)))

    return pick


def each(fn, *columns):
    return tuple(fn(*entry) for entry in zip(*columns))


def collide(f, v, w, s, tissue, stim):
    pick = typed(tissue)
    live = tissue > 0
    u = ((f[0] + f[1]) + (f[2] + f[3])) + ((f[4] + f[5]) + f[6])
    hv = 0.5 + 0.5 * jnp.tanh(25.0 * (u - 0.3))
    hw = 0.5 + 0.5 * jnp.tanh(25.0 * (u - 0.13))
    hm = 0.5 + 0.5 * jnp.tanh(25.0 * (u - pick(0.2, 0.1, 0.006)))
    ho = 0.5 + 0.5 * jnp.tanh(25.0 * (u - pick(0.006, 0.005, 0.006)))
    nv, nw, no = 1.0 - hv, 1.0 - hw, 1.0 - ho
    tv1, tv2 = (75.0, 80.0, 60.0), (10.0, 1.4506, 1150.0)
    tvm = pick(*tv1) + hm * pick(*each(lambda a, b: b - a, tv1, tv2))
    tw1, tw2 = (6.0, 70.0, 60.0), (140.0, 8.0, 15.0)
    thw = jnp.tanh(pick(200.0, 200.0, 65.0) * (u - pick(0.016, 0.016, 0.03)))
    twm = pick(*each(lambda a, b: (a + b) / 2, tw1, tw2)) + thw * pick(
        *each(lambda a, b: (b - a) / 2, tw1, tw2)
    )
    ts1, ts2 = (40.0, 91.0, 30.0181), (1.2, 0.8, 0.9957)
    tht = jnp.tanh(pick(2.0, 2.1, 2.0458) * (u - pick(0.65, 0.6, 0.65)))
    tso = pick(*each(lambda a, b: (a + b) / 2, ts1, ts2)) + tht * pick(
        *each(lambda a, b: (b - a) / 2, ts1, ts2)
    )
    ts = 2.7342 + hw * pick(*each(lambda a: a - 2.7342, (2.0, 4.0, 16.0)))
    to1, to2 = (470.0, 410.0, 400.0), (6.0, 7.0, 6.0)
    to = pick(*to1) + ho * pick(*each(lambda a, b: b - a, to1, to2))
    winf = no * (1.0 - u * pick(*each(lambda a: 1 / a, (0.0273, 0.01, 0.07)))) + ho * pick(
        0.78, 0.5, 0.94
    )
    minus_fi = v * hv * (u - 0.3) * (pick(1.56, 1.61, 1.55) - u) * pick(
        *each(lambda a: 1 / a, (0.1, 0.078, 0.11))
    )
    outward = u * nw / to + hw / tso
    minus_si = hw * w * s * pick(*each(lambda a: 1 / a, (2.9013, 3.3849, 1.8875)))
    react = stim + minus_fi - outward + minus_si
    dv = nv * (1.0 - hm - v) / tvm - hv * v * (1 / 1.4506)
    dw = nw * (winf - w) / twm - hw * w * pick(*each(lambda a: 1 / a, (280.0, 280.0, 200.0)))
    ds = ((0.5 + 0.5 * jnp.tanh(2.0994 * (u - 0.9087))) - s) / ts
    gates = (
        jnp.where(live, v + DT * dv, v),
        jnp.where(live, w + DT * dw, w),
        jnp.where(live, s + DT * ds, s),
    )
    rate = pick(*each(lambda a: 1 / a, (0.95, 0.8, 1.1)))
    keep = pick(*each(lambda a: 1 - 1 / a, (0.95, 0.8, 1.1)))
    share = 0.125 * (u * rate + DT * react)
    g = [jnp.where(live, f[0] * keep + 2.0 * share, DEAD)]
    for i in range(1, 7):
        g.append(jnp.where(live, f[i] * keep + share, DEAD))
    return g, gates


def kernel(
    f_hbm, g_hbm, x_hbm, t_hbm, s_hbm, amp, rc,
    fo_hbm, go_hbm, y_hbm, zt_ref, up_ref,
    fv, gv, xv, tv, sv, stim, cc, cxp, cxm, ysp, ysm, yrp, yrm, u1, u2, yv, red,
    load_sem, out_sem, hs_sem, hr_sem, as_sem, ar_sem,
):
    planes = fv.shape[1]
    quads = planes // 4
    slabs, tiles = lax.axis_size("slab"), lax.axis_size("tile")
    slab, tile = lax.axis_index("slab"), lax.axis_index("tile")
    core, yy, zz = lax.rem(tile, 2), lax.rem(tile // 2, 4), tile // 8

    loads = [
        pltpu.make_async_copy(src, dst, load_sem.at[i])
        for i, (src, dst) in enumerate(
            ((f_hbm, fv), (t_hbm, tv), (s_hbm, sv), (g_hbm, gv), (x_hbm, xv))
        )
    ]
    for copy in loads:
        copy.start()

    right = (lax.rem(slab + 1, slabs), tile)
    left = (lax.rem(slab + slabs - 1, slabs), tile)
    up = (slab, lax.rem(tile + 1, tiles))
    down = (slab, lax.rem(tile + tiles - 1, tiles))
    rank = (slab * 4 + yy, zz * 2 + core)

    def partner(stage, k):
        other = lax.rem(rank[stage] + k, GROUP)
        if stage == 0:
            return (other // 4, zz * 8 + lax.rem(other, 4) * 2 + core)
        return (slab, other // 2 * 8 + yy * 2 + lax.rem(other, 2))

    barrier = pltpu.get_barrier_semaphore()
    for dev in (right, left, up, down):
        pl.semaphore_signal(barrier, inc=1, device_id=dev, device_id_type=MESH)
    for stage in range(2):

        def greet(k, carry, stage=stage):
            pl.semaphore_signal(barrier, inc=1, device_id=partner(stage, k), device_id_type=MESH)
            return carry

        lax.fori_loop(1, GROUP, greet, 0)

    row4 = lax.broadcasted_iota(jnp.int32, (8, 128), 0)
    lane = lax.broadcasted_iota(jnp.int32, (4, 8, 128), 2)
    row = lax.broadcasted_iota(jnp.int32, (4, 8, 128), 1)
    yrow = lax.rem(row, 4)
    yrow2 = lax.rem(row4, 4)

    def store_collided(step, q, g):
        p = pl.ds(q * 4, 4)
        cc[0, p] = g[0]
        cc[1, p] = g[3]
        cc[2, p] = g[4]
        cc[3, p] = g[5]
        cc[4, p] = g[6]
        cxp[step, pl.ds(q * 4 + 1, 4)] = g[1]
        cxm[step, p] = g[2]
        face_p = g[3][3]
        face_m = g[4][0]
        for k in range(3):
            face_p = jnp.where(yrow2 == k, pltpu.roll(g[3][k], 5 + k, 0), face_p)
        for k in range(1, 4):
            face_m = jnp.where(yrow2 == k, pltpu.roll(g[4][k], k, 0), face_m)
        ysp[step, q] = face_p
        ysm[step, q] = face_m

    def halos(step):
        pairs = (
            (cxp.at[step, pl.ds(planes, 1)], cxp.at[step, pl.ds(0, 1)], right),
            (cxm.at[step, pl.ds(0, 1)], cxm.at[step, pl.ds(planes, 1)], left),
            (ysp.at[step], yrp.at[step], up),
            (ysm.at[step], yrm.at[step], down),
        )
        return [
            pltpu.make_async_remote_copy(
                src_ref=src,
                dst_ref=dst,
                send_sem=hs_sem.at[step * 4 + i],
                recv_sem=hr_sem.at[step * 4 + i],
                device_id=dev,
                device_id_type=MESH,
            )
            for i, (src, dst, dev) in enumerate(pairs)
        ]

    def settle_halos(step):
        for copy in halos(step):
            copy.wait_recv()
        cxp[step, pl.ds(0, 1)] = jnp.where(slab == 0, DEAD, cxp[step, pl.ds(0, 1)])
        cxm[step, pl.ds(planes, 1)] = jnp.where(
            slab == slabs - 1, DEAD, cxm[step, pl.ds(planes, 1)]
        )
        yrp[step] = jnp.where(tile == 0, DEAD, yrp[step])
        yrm[step] = jnp.where(tile == tiles - 1, DEAD, yrm[step])

    def propagate(step, q, tissue):
        p = pl.ds(q * 4, 4)
        p1 = pl.ds(q * 4 + 1, 4)

        def bounce(moved, back):
            return jnp.where(moved > LIMIT, moved, back)

        gx1, gx2 = cxp[step, p1], cxm[step, p]
        gy1, gy2, gz1, gz2 = cc[1, p], cc[2, p], cc[3, p], cc[4, p]
        hp, hm = yrp[step, q], yrm[step, q]
        halo_p = jnp.stack([hp] + [pltpu.roll(hp, 8 - k, 0) for k in range(1, 4)])
        halo_m = jnp.stack([pltpu.roll(hm, 3 - k, 0) for k in range(3)] + [hm])
        my1 = jnp.where(yrow == 0, halo_p, pltpu.roll(gy1, 1, 1))
        my2 = jnp.where(yrow == 3, halo_m, pltpu.roll(gy2, 7, 1))
        rz1 = pltpu.roll(gz1, 1, 2)
        rz2 = pltpu.roll(gz2, 127, 2)
        mz1 = jnp.where(lane == 0, jnp.where(row >= 4, pltpu.roll(rz1, 4, 1), DEAD), rz1)
        mz2 = jnp.where(lane == 127, jnp.where(row < 4, pltpu.roll(rz2, 4, 1), DEAD), rz2)
        f = (
            cc[0, p],
            bounce(cxp[step, p], gx2),
            bounce(cxm[step, p1], gx1),
            bounce(my1, gy2),
            bounce(my2, gy1),
            bounce(mz1, gz2),
            bounce(mz2, gz1),
        )
        live = tissue > 0
        f = [jnp.where(live, part, 0.0) for part in f]
        u = ((f[0] + f[1]) + (f[2] + f[3])) + ((f[4] + f[5]) + f[6])
        return f, u

    def advance(q, f, current):
        p = pl.ds(q * 4, 4)
        g, gates = collide(f, gv[0, p], gv[1, p], gv[2, p], tv[p], current)
        for i in range(3):
            gv[i, p] = gates[i]
        return g

    def reduce_copy(which, stage, k):
        at = (which * 2 + stage) * GROUP
        slot = red.at[at + rank[stage]]
        return pltpu.make_async_remote_copy(
            src_ref=slot,
            dst_ref=slot,
            send_sem=as_sem.at[at + k],
            recv_sem=ar_sem.at[at + k],
            device_id=partner(stage, k),
            device_id_type=MESH,
        )

    def reduce_send(which, stage, block):
        red[(which * 2 + stage) * GROUP + rank[stage]] = block

        def send(k, carry):
            reduce_copy(which, stage, k).start()
            return carry

        lax.fori_loop(1, GROUP, send, 0)

    def reduce_sum(which, stage):
        def take(k, carry):
            reduce_copy(which, stage, k).wait_recv()
            return carry

        lax.fori_loop(1, GROUP, take, 0)
        at = (which * 2 + stage) * GROUP
        parts = [red[at + i] for i in range(GROUP)]
        while len(parts) > 1:
            parts = [a + b for a, b in zip(parts[::2], parts[1::2])]
        return parts[0]

    def packed(m):
        return jnp.concatenate([m[8 * b : 8 * b + 8] for b in range(4)], axis=1)

    def unpacked(m):
        return jnp.concatenate([m[:, 32 * b : 32 * b + 32] for b in range(4)], axis=0)

    ri = lax.broadcasted_iota(jnp.int32, (32, 32), 0)
    ci = lax.broadcasted_iota(jnp.int32, (32, 32), 1)

    def eliminate(gram):
        m = jnp.concatenate([gram, jnp.where(ri == ci, 1.0, 0.0)], axis=1)
        below = lax.broadcasted_iota(jnp.int32, (32, 64), 0)
        for j in range(31):
            scaled = m[j : j + 1, :] / m[j : j + 1, j : j + 1]
            m = m - jnp.where(below > j, m[:, j : j + 1] * scaled, 0.0)
        upper = m[:, :32]
        pivot = jnp.sum(jnp.where(ri == ci, upper, 0.0), axis=1, keepdims=True)
        scale = 1.0 / jnp.sqrt(pivot)
        return jnp.where(ri <= ci, upper * scale, 0.0), m[:, 32:] * scale

    def thirds(a):
        hi = a.astype(BF16)
        rest = a - hi.astype(F32)
        mid = rest.astype(BF16)
        return hi, mid, (rest - mid.astype(F32)).astype(BF16)

    for copy in loads[:4]:
        copy.wait()

    def first(q, carry):
        p = pl.ds(q * 4, 4)
        site = sv[p]
        current = jnp.zeros((4, 8, 128), F32)
        for k in range(8):
            current = jnp.where(site == k + 1, amp[k], current)
        stim[p] = current
        store_collided(0, q, advance(q, [fv[i, p] for i in range(7)], current))
        return carry

    lax.fori_loop(0, quads, first, 0)
    pl.semaphore_wait(barrier, 4 + 2 * (GROUP - 1))
    for copy in halos(0):
        copy.start()

    loads[4].wait()
    rows = planes * 8

    def old_gram(x, acc):
        chunk = jnp.concatenate(
            [xv[pl.ds(x * 8 + r, 32, stride=rows), :] for r in range(8)], axis=1
        )
        hi = chunk.astype(BF16)
        lo = (chunk - hi.astype(F32)).astype(BF16)
        both = jnp.concatenate([hi, lo], axis=0)
        return acc + lax.dot_general(both, both, NT, preferred_element_type=F32)

    acc = lax.fori_loop(0, planes, old_gram, jnp.zeros((64, 64), F32))
    reduce_send(0, 0, packed(acc[:32, :32] + acc[:32, 32:] + acc[32:, :32] + acc[32:, 32:]))

    settle_halos(0)

    def second(q, carry):
        p = pl.ds(q * 4, 4)
        f, u = propagate(0, q, tv[p])
        u1[p] = u
        for i in range(7):
            fv[i, p] = f[i]
        return carry

    lax.fori_loop(0, quads, second, 0)

    def third(q, carry):
        p = pl.ds(q * 4, 4)
        store_collided(1, q, advance(q, [fv[i, p] for i in range(7)], stim[p]))
        return carry

    lax.fori_loop(0, quads, third, 0)
    for copy in halos(1):
        copy.start()
    reduce_send(0, 1, reduce_sum(0, 0))
    gates_out = pltpu.make_async_copy(gv, go_hbm, out_sem.at[0])
    gates_out.start()

    settle_halos(1)

    def fourth(q, carry):
        p = pl.ds(q * 4, 4)
        f, u = propagate(1, q, tv[p])
        u2[p] = u
        for i in range(7):
            fv[i, p] = f[i]
        return carry

    lax.fori_loop(0, quads, fourth, 0)
    f_out = pltpu.make_async_copy(fv, fo_hbm, out_sem.at[1])
    f_out.start()

    gram = unpacked(reduce_sum(0, 1))
    taken = (ri == rc[0]) | (ri == rc[1]) | (ci == rc[0]) | (ci == rc[1])
    gram = jnp.where(taken, jnp.where(ri == ci, 1.0, 0.0), gram)
    r0, t0 = eliminate(gram)
    th, tm, tl = thirds(t0)
    wide = jnp.concatenate([th, th, tm, th, tm, tl], axis=1)

    column = lax.broadcasted_iota(jnp.int32, (32, 128), 0)
    is1, is2 = column == rc[0], column == rc[1]

    def new_gram(x, acc):
        pieces = []
        for r in range(8):
            piece = xv[pl.ds(x * 8 + r, 32, stride=rows), :]
            piece = jnp.where(is1, u1[x, r : r + 1, :], piece)
            pieces.append(jnp.where(is2, u2[x, r : r + 1, :], piece))
        hi, mid, lo = thirds(jnp.concatenate(pieces, axis=1))
        tall = jnp.concatenate([hi, mid, hi, lo, mid, hi], axis=0)
        y = jnp.dot(wide, tall, preferred_element_type=F32)
        for r in range(8):
            yv[x * 8 + r] = y[:, 128 * r : 128 * r + 128]
        parts = jnp.concatenate(thirds(y), axis=0)
        return acc + lax.dot_general(parts, parts, NT, preferred_element_type=F32)

    acc = lax.fori_loop(0, planes, new_gram, jnp.zeros((96, 96), F32))
    a, b, c = (acc[32 * i : 32 * i + 32] for i in range(3))
    gram = a[:, :32] + ((a[:, 32:64] + b[:, :32]) + (b[:, 32:64] + (a[:, 64:] + c[:, :32])))
    reduce_send(1, 0, packed(gram))
    y_out = pltpu.make_async_copy(yv, y_hbm, out_sem.at[2])
    y_out.start()
    reduce_send(1, 1, reduce_sum(1, 0))
    r2, z2 = eliminate(unpacked(reduce_sum(1, 1)))
    norm = math.sqrt(planes * 1024 * slabs * tiles)
    zt_ref[...] = z2 * norm
    up_ref[...] = jnp.dot(
        r2, r0, precision=lax.Precision.HIGHEST, preferred_element_type=F32
    ) * (1.0 / norm)

    gates_out.wait()
    f_out.wait()
    y_out.wait()
    for step in range(2):
        for copy in halos(step):
            copy.wait_send()
    for which in range(2):
        for stage in range(2):

            def sent(k, carry, which=which, stage=stage):
                reduce_copy(which, stage, k).wait_send()
                return carry

            lax.fori_loop(1, GROUP, sent, 0)


def basis_kernel(y_ref, f_ref, g_ref, z_ref, r_ref, q_ref, fo_ref, go_ref, ro_ref):
    z = z_ref[...]
    zh = z.astype(BF16)
    zl = (z - zh.astype(F32)).astype(BF16)
    wide = jnp.concatenate([zh, zh, zl], axis=1)
    for x in range(y_ref.shape[0] // 8):
        chunk = jnp.concatenate([y_ref[x * 8 + r] for r in range(8)], axis=1)
        hi = chunk.astype(BF16)
        lo = (chunk - hi.astype(F32)).astype(BF16)
        q = jnp.dot(wide, jnp.concatenate([hi, lo, hi], axis=0), preferred_element_type=F32)
        for r in range(8):
            q_ref[:, x * 8 + r, :] = q[:, 128 * r : 128 * r + 128]
    fo_ref[...] = f_ref[...]
    go_ref[...] = g_ref[...]
    ro_ref[...] = r_ref[...]


def local(distributions, gate_states, history, tissue, stim_site, stim_amp, record_column):
    planes = distributions.shape[1]
    rows = planes * 8
    any_space = pl.BlockSpec(memory_space=pl.ANY)
    smem = pl.BlockSpec(memory_space=pltpu.SMEM)
    vmem = pl.BlockSpec(memory_space=pltpu.VMEM)
    grid_f = (7, planes, 8, 128)
    shapes = [
        jax.ShapeDtypeStruct(grid_f, F32),
        jax.ShapeDtypeStruct((3, planes, 8, 128), F32),
        jax.ShapeDtypeStruct((rows, 32, 128), F32),
        jax.ShapeDtypeStruct((32, 32), F32),
        jax.ShapeDtypeStruct((32, 32), F32),
    ]
    plane = (planes, 8, 128)
    scratch = [
        pltpu.VMEM(grid_f, F32),
        pltpu.VMEM((3,) + plane, F32),
        pltpu.VMEM((32 * rows, 128), F32),
        pltpu.VMEM(plane, jnp.int32),
        pltpu.VMEM(plane, jnp.int32),
        pltpu.VMEM(plane, F32),
        pltpu.VMEM((5,) + plane, F32),
        pltpu.VMEM((2, planes + 1, 8, 128), F32),
        pltpu.VMEM((2, planes + 1, 8, 128), F32),
        pltpu.VMEM((2, planes // 4, 8, 128), F32),
        pltpu.VMEM((2, planes // 4, 8, 128), F32),
        pltpu.VMEM((2, planes // 4, 8, 128), F32),
        pltpu.VMEM((2, planes // 4, 8, 128), F32),
        pltpu.VMEM(plane, F32),
        pltpu.VMEM(plane, F32),
        pltpu.VMEM((rows, 32, 128), F32),
        pltpu.VMEM((4 * GROUP, 8, 128), F32),
        pltpu.SemaphoreType.DMA((5,)),
        pltpu.SemaphoreType.DMA((3,)),
        pltpu.SemaphoreType.DMA((8,)),
        pltpu.SemaphoreType.DMA((8,)),
        pltpu.SemaphoreType.DMA((4 * GROUP,)),
        pltpu.SemaphoreType.DMA((4 * GROUP,)),
    ]
    f, g, y, zt, up = pl.pallas_call(
        kernel,
        out_shape=shapes,
        in_specs=[any_space] * 5 + [smem] * 2,
        out_specs=[any_space] * 3 + [vmem] * 2,
        scratch_shapes=scratch,
        compiler_params=pltpu.CompilerParams(
            collective_id=0, has_side_effects=True, vmem_limit_bytes=58 << 20
        ),
    )(
        split_rows(distributions, grid_f),
        split_rows(gate_states, (3,) + plane),
        split_rows(history, (32 * rows, 128)),
        split_rows(tissue, plane),
        split_rows(stim_site, plane),
        stim_amp,
        record_column,
    )
    part = 32
    q, f, g, up = pl.pallas_call(
        basis_kernel,
        grid=(rows // part,),
        out_shape=[
            jax.ShapeDtypeStruct((32, rows, 128), F32),
            jax.ShapeDtypeStruct((7, rows, 128), F32),
            jax.ShapeDtypeStruct((3, rows, 128), F32),
            jax.ShapeDtypeStruct((32, 32), F32),
        ],
        in_specs=[
            pl.BlockSpec((part, 32, 128), lambda i: (i, 0, 0)),
            pl.BlockSpec((7, part, 128), lambda i: (0, i, 0)),
            pl.BlockSpec((3, part, 128), lambda i: (0, i, 0)),
            pl.BlockSpec((32, 32), lambda i: (0, 0)),
            pl.BlockSpec((32, 32), lambda i: (0, 0)),
        ],
        out_specs=[
            pl.BlockSpec((32, part, 128), lambda i: (0, i, 0)),
            pl.BlockSpec((7, part, 128), lambda i: (0, i, 0)),
            pl.BlockSpec((3, part, 128), lambda i: (0, i, 0)),
            pl.BlockSpec((32, 32), lambda i: (0, 0)),
        ],
        compiler_params=pltpu.CompilerParams(vmem_limit_bytes=58 << 20),
    )(y, f.reshape(7, rows, 128), g.reshape(3, rows, 128), zt, up)
    return (
        join_rows(f, distributions.shape),
        join_rows(g, gate_states.shape),
        join_rows(q, history.shape),
        up,
    )


def solution(mesh):
    field = P(None, "slab", "tile", None)
    label = P("slab", "tile", None)
    return jax.shard_map(
        local,
        mesh=mesh,
        in_specs=(field, field, field, label, label, P(), P()),
        out_specs=(field, field, field, P()),
        check_vma=False,
    )
```

profile of v0, /device:TPU:1, one launch (start us, length us, event | category | flops | bytes accessed | tf_op | source)
XLA Modules:
  0.0 69.0 jit_solution(15777330416788238399)
XLA Ops:
  0.6 59.8 %shard_map.102 = (f32[7,32,8,128]{3,2,1,0:T(8,128)}, f32[3,32,8,128]{3,2,1,0:T(8,128)}, f32[256,32,128]{2,1,0:T(8,128)}, f32[32,32]{1,0:T(8,128)}, f32[32,32]{1,0:T(8,128)}) custom-call(f32[7,32,8,128]{3,2,1,0:T(8,128)} %bitcast.43, f32[3,32,8,128]{3,2,1,0:T(8,128)} %bitcast.45, f32[8192,128]{1,0:T(8,128)} %bitcast.42, s32[32,8,128]{2,1,0:T(8,128)} %bitcast.47, ...), custom_call_target="tpu_custom_call" | custom-call | tf_op jit(solution)/shard_map/pallas_call | solution.py:482
  60.5 8.6 %shard_map.103 = (f32[32,256,128]{2,1,0:T(8,128)}, f32[7,256,128]{2,1,0:T(8,128)}, f32[3,256,128]{2,1,0:T(8,128)}, f32[32,32]{1,0:T(8,128)}) custom-call(f32[256,32,128]{2,1,0:T(8,128)} %get-tuple-element.13.y_ref, f32[7,256,128]{2,1,0:T(8,128)} %bitcast.44, f32[3,256,128]{2,1,0:T(8,128)} %bitcast.46, f32[32,32]{1,0:T(8,128)} %get-tuple-element.16.z_ref, ...), custom_call_target="tpu_custom_call" | custom-call | tf_op jit(solution)/shard_map/pallas_call | solution.py:501
where the time goes:
time: 69.3 us; the launch traced here: 69 us
  Pallas kernels  68.4 us (99%)
    pallas_call x1, Pallas kernels, local(): pl.pallas_call(kernel, out_shape=shapes, in_specs=[any_space] * 5 + [smem...  59.8 us
    pallas_call x1, Pallas kernels, local(): pl.pallas_call(basis_kernel, grid=(rows // part,), out_shape=[jax.ShapeDt...  8.57 us

commit v1 on v0

--- a/solution.py
+++ b/solution.py
@@ -16,6 +16,7 @@
 BF16 = jnp.bfloat16
 NT = (((1,), (1,)), ((), ()))
 GROUP = 16
+PANEL = 4
 
 
 def split_rows(a, shape):
@@ -104,9 +105,10 @@
 
 def kernel(
     f_hbm, g_hbm, x_hbm, t_hbm, s_hbm, amp, rc,
-    fo_hbm, go_hbm, y_hbm, zt_ref, up_ref,
-    fv, gv, xv, tv, sv, stim, cc, cxp, cxm, ysp, ysm, yrp, yrm, u1, u2, yv, red,
-    load_sem, out_sem, hs_sem, hr_sem, as_sem, ar_sem,
+    f_out, g_out, y_out, zt_ref, up_ref,
+    fv, gv, xv, tv, sv, stim, cc, cxp, cxm, ysp, ysm, yrp, yrm, u1, u2,
+    xs, acc1, acc2, red,
+    load_sem, hs_sem, hr_sem, as_sem, ar_sem,
 ):
     planes = fv.shape[1]
     quads = planes // 4
@@ -117,7 +119,7 @@
     loads = [
         pltpu.make_async_copy(src, dst, load_sem.at[i])
         for i, (src, dst) in enumerate(
-            ((f_hbm, fv), (t_hbm, tv), (s_hbm, sv), (g_hbm, gv), (x_hbm, xv))
+            ((x_hbm, xv), (f_hbm, fv), (t_hbm, tv), (s_hbm, sv), (g_hbm, gv))
         )
     ]
     for copy in loads:
@@ -231,40 +233,36 @@
         u = ((f[0] + f[1]) + (f[2] + f[3])) + ((f[4] + f[5]) + f[6])
         return f, u
 
-    def advance(q, f, current):
+    def advance(q, f, current, gates_to):
         p = pl.ds(q * 4, 4)
         g, gates = collide(f, gv[0, p], gv[1, p], gv[2, p], tv[p], current)
         for i in range(3):
-            gv[i, p] = gates[i]
+            gates_to[i, p] = gates[i]
         return g
 
-    def reduce_copy(which, stage, k):
-        at = (which * 2 + stage) * GROUP
-        slot = red.at[at + rank[stage]]
+    def reduce_copy(which, stage, slot, k):
         return pltpu.make_async_remote_copy(
             src_ref=slot,
             dst_ref=slot,
-            send_sem=as_sem.at[at + k],
-            recv_sem=ar_sem.at[at + k],
+            send_sem=as_sem.at[which * 2 + stage],
+            recv_sem=ar_sem.at[which * 2 + stage],
             device_id=partner(stage, k),
             device_id_type=MESH,
         )
 
     def reduce_send(which, stage, block):
-        red[(which * 2 + stage) * GROUP + rank[stage]] = block
-
-        def send(k, carry):
-            reduce_copy(which, stage, k).start()
-            return carry
-
-        lax.fori_loop(1, GROUP, send, 0)
+        at = (which * 2 + stage) * GROUP + rank[stage]
+        red[at] = block
+        for k in range(1, GROUP):
+            reduce_copy(which, stage, red.at[at], k).start()
+
+    def reduce_all(which, stage):
+        return reduce_copy(
+            which, stage, red.at[pl.ds((which * 2 + stage) * GROUP, GROUP - 1)], 1
+        )
 
     def reduce_sum(which, stage):
-        def take(k, carry):
-            reduce_copy(which, stage, k).wait_recv()
-            return carry
-
-        lax.fori_loop(1, GROUP, take, 0)
+        reduce_all(which, stage).wait_recv()
         at = (which * 2 + stage) * GROUP
         parts = [red[at + i] for i in range(GROUP)]
         while len(parts) > 1:
@@ -280,24 +278,58 @@
     ri = lax.broadcasted_iota(jnp.int32, (32, 32), 0)
     ci = lax.broadcasted_iota(jnp.int32, (32, 32), 1)
 
-    def eliminate(gram):
-        m = jnp.concatenate([gram, jnp.where(ri == ci, 1.0, 0.0)], axis=1)
+    eye = jnp.where(ri == ci, 1.0, 0.0)
+
+    def eliminate(a):
+        m = jnp.concatenate([a, eye], axis=1)
         below = lax.broadcasted_iota(jnp.int32, (32, 64), 0)
-        for j in range(31):
-            scaled = m[j : j + 1, :] / m[j : j + 1, j : j + 1]
-            m = m - jnp.where(below > j, m[:, j : j + 1] * scaled, 0.0)
+        for p in range(0, 32, PANEL):
+            cols = [jnp.broadcast_to(m[:, p + k : p + k + 1], (32, 64)) for k in range(PANEL)]
+            rows = [m[p + k : p + k + 1, :] for k in range(PANEL)]
+            taken_off = 0.0
+            for k in range(PANEL):
+                j = p + k
+                low = jnp.where(below > j, cols[k] * (1.0 / cols[k][j : j + 1, :]), 0.0)
+                for q in range(k + 1, PANEL):
+                    cols[q] = cols[q] - low * cols[q][j : j + 1, :]
+                    rows[q] = rows[q] - low[p + q : p + q + 1, :] * rows[k]
+                taken_off = taken_off + low * rows[k]
+            m = m - taken_off
         upper = m[:, :32]
         pivot = jnp.sum(jnp.where(ri == ci, upper, 0.0), axis=1, keepdims=True)
-        scale = 1.0 / jnp.sqrt(pivot)
-        return jnp.where(ri <= ci, upper * scale, 0.0), m[:, 32:] * scale
-
-    def thirds(a):
-        hi = a.astype(BF16)
-        rest = a - hi.astype(F32)
-        mid = rest.astype(BF16)
-        return hi, mid, (rest - mid.astype(F32)).astype(BF16)
-
-    for copy in loads[:4]:
+        return jnp.where(ri <= ci, upper, 0.0), m[:, 32:], pivot
+
+    wide_row = lax.broadcasted_iota(jnp.int32, (256, 256), 0)
+    wide_col = lax.broadcasted_iota(jnp.int32, (256, 256), 1)
+    same = lax.rem(wide_row, 8) == lax.rem(wide_col, 8)
+
+    def folded(p):
+        m = jnp.sum(jnp.where(same, p, 0.0).reshape(32, 8, 256), axis=1)
+        place = lax.broadcasted_iota(jnp.int32, (256, 32), 0) // 8
+        pick = jnp.where(place == lax.broadcasted_iota(jnp.int32, (256, 32), 1), 1.0, 0.0)
+        return jnp.dot(m, pick, precision=lax.Precision.HIGHEST, preferred_element_type=F32)
+
+    loads[0].wait()
+
+    def pair(x):
+        return jnp.concatenate([xv[:, 2 * x].reshape(256, 128), xv[:, 2 * x + 1].reshape(256, 128)], axis=1)
+
+    acc1[...] = jnp.zeros((256, 256), F32)
+
+    def old_gram(i, carry):
+        parts = [pair(2 * i + k).astype(BF16) for k in range(2)]
+        for k in range(2):
+            xs[2 * i + k, :256] = parts[k]
+        hi = jnp.concatenate(parts, axis=1)
+        acc1[...] += lax.dot_general(hi, hi, NT, preferred_element_type=F32)
+        return carry
+
+    lax.fori_loop(0, quads, old_gram, 0)
+    block = packed(folded(acc1[...]))
+    pl.semaphore_wait(barrier, 4 + 2 * (GROUP - 1))
+    reduce_send(0, 0, block)
+
+    for copy in loads[1:]:
         copy.wait()
 
     def first(q, carry):
@@ -307,28 +339,23 @@
         for k in range(8):
             current = jnp.where(site == k + 1, amp[k], current)
         stim[p] = current
-        store_collided(0, q, advance(q, [fv[i, p] for i in range(7)], current))
+        store_collided(0, q, advance(q, [fv[i, p] for i in range(7)], current, gv))
         return carry
 
     lax.fori_loop(0, quads, first, 0)
-    pl.semaphore_wait(barrier, 4 + 2 * (GROUP - 1))
     for copy in halos(0):
         copy.start()
 
-    loads[4].wait()
-    rows = planes * 8
-
-    def old_gram(x, acc):
-        chunk = jnp.concatenate(
-            [xv[pl.ds(x * 8 + r, 32, stride=rows), :] for r in range(8)], axis=1
-        )
-        hi = chunk.astype(BF16)
-        lo = (chunk - hi.astype(F32)).astype(BF16)
-        both = jnp.concatenate([hi, lo], axis=0)
-        return acc + lax.dot_general(both, both, NT, preferred_element_type=F32)
-
-    acc = lax.fori_loop(0, planes, old_gram, jnp.zeros((64, 64), F32))
-    reduce_send(0, 0, packed(acc[:32, :32] + acc[:32, 32:] + acc[32:, :32] + acc[32:, 32:]))
+    def finer(i, carry):
+        rest = pair(i) - xs[i, :256].astype(F32)
+        mid = rest.astype(BF16)
+        xs[i, 256:512] = mid
+        xs[i, 512:] = (rest - mid.astype(F32)).astype(BF16)
+        return carry
+
+    lax.fori_loop(0, planes // 2, finer, 0)
+
+    reduce_send(0, 1, reduce_sum(0, 0))
 
     settle_halos(0)
 
@@ -336,23 +363,20 @@
         p = pl.ds(q * 4, 4)
         f, u = propagate(0, q, tv[p])
         u1[p] = u
-        for i in range(7):
-            fv[i, p] = f[i]
+        store_collided(1, q, advance(q, f, stim[p], g_out))
         return carry
 
     lax.fori_loop(0, quads, second, 0)
-
-    def third(q, carry):
-        p = pl.ds(q * 4, 4)
-        store_collided(1, q, advance(q, [fv[i, p] for i in range(7)], stim[p]))
-        return carry
-
-    lax.fori_loop(0, quads, third, 0)
     for copy in halos(1):
         copy.start()
-    reduce_send(0, 1, reduce_sum(0, 0))
-    gates_out = pltpu.make_async_copy(gv, go_hbm, out_sem.at[0])
-    gates_out.start()
+
+    gram = unpacked(reduce_sum(0, 1))
+    taken = (ri == rc[0]) | (ri == rc[1]) | (ci == rc[0]) | (ci == rc[1])
+    gram = jnp.where(taken, eye, gram * (1.0 + eye * 2.0**-16))
+    _, inv0, pivot = eliminate(gram)
+    t0 = (inv0 * (1.0 / jnp.sqrt(pivot))).astype(BF16)
+    spread = spread_rows(t0)
+    spread = jnp.concatenate([spread, spread, spread], axis=1)
 
     settle_halos(1)
 
@@ -361,103 +385,127 @@
         f, u = propagate(1, q, tv[p])
         u2[p] = u
         for i in range(7):
-            fv[i, p] = f[i]
+            f_out[i, p] = f[i]
         return carry
 
     lax.fori_loop(0, quads, fourth, 0)
-    f_out = pltpu.make_async_copy(fv, fo_hbm, out_sem.at[1])
-    f_out.start()
-
-    gram = unpacked(reduce_sum(0, 1))
-    taken = (ri == rc[0]) | (ri == rc[1]) | (ci == rc[0]) | (ci == rc[1])
-    gram = jnp.where(taken, jnp.where(ri == ci, 1.0, 0.0), gram)
-    r0, t0 = eliminate(gram)
-    th, tm, tl = thirds(t0)
-    wide = jnp.concatenate([th, th, tm, th, tm, tl], axis=1)
-
-    column = lax.broadcasted_iota(jnp.int32, (32, 128), 0)
+
+    column = lax.broadcasted_iota(jnp.int32, (32, 8, 256), 0)
     is1, is2 = column == rc[0], column == rc[1]
-
-    def new_gram(x, acc):
-        pieces = []
-        for r in range(8):
-            piece = xv[pl.ds(x * 8 + r, 32, stride=rows), :]
-            piece = jnp.where(is1, u1[x, r : r + 1, :], piece)
-            pieces.append(jnp.where(is2, u2[x, r : r + 1, :], piece))
-        hi, mid, lo = thirds(jnp.concatenate(pieces, axis=1))
-        tall = jnp.concatenate([hi, mid, hi, lo, mid, hi], axis=0)
-        y = jnp.dot(wide, tall, preferred_element_type=F32)
-        for r in range(8):
-            yv[x * 8 + r] = y[:, 128 * r : 128 * r + 128]
-        parts = jnp.concatenate(thirds(y), axis=0)
-        return acc + lax.dot_general(parts, parts, NT, preferred_element_type=F32)
-
-    acc = lax.fori_loop(0, planes, new_gram, jnp.zeros((96, 96), F32))
-    a, b, c = (acc[32 * i : 32 * i + 32] for i in range(3))
-    gram = a[:, :32] + ((a[:, 32:64] + b[:, :32]) + (b[:, 32:64] + (a[:, 64:] + c[:, :32])))
+    acc1[...] = jnp.zeros((256, 256), F32)
+    acc2[...] = jnp.zeros((256, 256), F32)
+
+    def whitened(i):
+        y = jnp.dot(spread, xs[i], preferred_element_type=F32)
+        new1 = jnp.concatenate([u1[2 * i], u1[2 * i + 1]], axis=1)
+        new2 = jnp.concatenate([u2[2 * i], u2[2 * i + 1]], axis=1)
+        y = jnp.where(is1, new1[None], jnp.where(is2, new2[None], y.reshape(32, 8, 256)))
+        y = y.reshape(256, 256)
+        hi = y.astype(BF16)
+        lo = (y - hi.astype(F32)).astype(BF16)
+        y_out[i, 0] = hi
+        y_out[i, 1] = lo
+        return hi, lo
+
+    def new_gram(i, carry):
+        (h1, l1), (h2, l2) = whitened(2 * i), whitened(2 * i + 1)
+        every = jnp.concatenate([h1, h2, l1, l2], axis=1)
+        acc1[...] += lax.dot_general(every, every, NT, preferred_element_type=F32)
+        acc2[...] += lax.dot_general(
+            every[:, :512], every[:, 512:], NT, preferred_element_type=F32
+        )
+        return carry
+
+    lax.fori_loop(0, quads, new_gram, 0)
+    cross = folded(acc2[...])
+    gram = folded(acc1[...]) + (
+        cross
+        + lax.dot_general(
+            eye, cross, NT, precision=lax.Precision.HIGHEST, preferred_element_type=F32
+        )
+    )
     reduce_send(1, 0, packed(gram))
-    y_out = pltpu.make_async_copy(yv, y_hbm, out_sem.at[2])
-    y_out.start()
+    _, inv0, pivot = eliminate(t0.astype(F32))
+    back = inv0 * (1.0 / pivot)
     reduce_send(1, 1, reduce_sum(1, 0))
-    r2, z2 = eliminate(unpacked(reduce_sum(1, 1)))
+    r2, inv2, pivot = eliminate(unpacked(reduce_sum(1, 1)))
+    scale = 1.0 / jnp.sqrt(pivot)
     norm = math.sqrt(planes * 1024 * slabs * tiles)
-    zt_ref[...] = z2 * norm
-    up_ref[...] = jnp.dot(
-        r2, r0, precision=lax.Precision.HIGHEST, preferred_element_type=F32
+    zt_ref[...] = inv2 * (scale * norm)
+    up_ref[...] = lax.dot_general(
+        r2 * scale, back, NT, precision=lax.Precision.HIGHEST, preferred_element_type=F32
     ) * (1.0 / norm)
 
-    gates_out.wait()
-    f_out.wait()
-    y_out.wait()
     for step in range(2):
         for copy in halos(step):
             copy.wait_send()
     for which in range(2):
         for stage in range(2):
-
-            def sent(k, carry, which=which, stage=stage):
-                reduce_copy(which, stage, k).wait_send()
-                return carry
-
-            lax.fori_loop(1, GROUP, sent, 0)
-
-
-def basis_kernel(y_ref, f_ref, g_ref, z_ref, r_ref, q_ref, fo_ref, go_ref, ro_ref):
+            reduce_all(which, stage).wait_send()
+
+
+def spread_rows(t):
+    place = lax.broadcasted_iota(jnp.int32, (256, 32), 0) // 8
+    pick = jnp.where(place == lax.broadcasted_iota(jnp.int32, (256, 32), 1), 1.0, 0.0).astype(BF16)
+    half = jnp.dot(pick, t, preferred_element_type=F32).astype(BF16)
+    full = lax.dot_general(half, pick, NT, preferred_element_type=F32)
+    row = lax.rem(lax.broadcasted_iota(jnp.int32, (256, 256), 0), 8)
+    col = lax.rem(lax.broadcasted_iota(jnp.int32, (256, 256), 1), 8)
+    return jnp.where(row == col, full, 0.0).astype(BF16)
+
+
+def basis_kernel(
+    y_ref, f_ref, g_ref, z_ref, r_ref, q_hbm, f_hbm, g_hbm, r_hbm, qv, q_sem, p_sem
+):
+    parts = q_sem.shape[0]
+    pairs = y_ref.shape[0] // parts
+    passed = [
+        pltpu.make_async_copy(src, dst, p_sem.at[i])
+        for i, (src, dst) in enumerate(((f_ref, f_hbm), (g_ref, g_hbm), (r_ref, r_hbm)))
+    ]
+    for copy in passed:
+        copy.start()
     z = z_ref[...]
-    zh = z.astype(BF16)
-    zl = (z - zh.astype(F32)).astype(BF16)
-    wide = jnp.concatenate([zh, zh, zl], axis=1)
-    for x in range(y_ref.shape[0] // 8):
-        chunk = jnp.concatenate([y_ref[x * 8 + r] for r in range(8)], axis=1)
-        hi = chunk.astype(BF16)
-        lo = (chunk - hi.astype(F32)).astype(BF16)
-        q = jnp.dot(wide, jnp.concatenate([hi, lo, hi], axis=0), preferred_element_type=F32)
-        for r in range(8):
-            q_ref[:, x * 8 + r, :] = q[:, 128 * r : 128 * r + 128]
-    fo_ref[...] = f_ref[...]
-    go_ref[...] = g_ref[...]
-    ro_ref[...] = r_ref[...]
+    hi = z.astype(BF16)
+    spread = spread_rows(hi)
+    rest = spread_rows((z - hi.astype(F32)).astype(BF16))
+    wide = jnp.concatenate([spread, spread, rest], axis=1)
+    stores = []
+    for i in range(parts):
+        for k in range(pairs):
+            at = i * pairs + k
+            tall = jnp.concatenate([y_ref[at, 0], y_ref[at, 1], y_ref[at, 0]], axis=0)
+            q = jnp.dot(wide, tall, preferred_element_type=F32)
+            for j in range(2):
+                qv[:, 2 * at + j] = q[:, 128 * j : 128 * j + 128].reshape(32, 8, 128)
+        planes = pl.ds(2 * i * pairs, 2 * pairs)
+        stores.append(
+            pltpu.make_async_copy(qv.at[:, planes], q_hbm.at[:, planes], q_sem.at[i])
+        )
+        stores[-1].start()
+    for copy in passed + stores:
+        copy.wait()
 
 
 def local(distributions, gate_states, history, tissue, stim_site, stim_amp, record_column):
     planes = distributions.shape[1]
-    rows = planes * 8
+    hbm = pl.BlockSpec(memory_space=pltpu.HBM)
     any_space = pl.BlockSpec(memory_space=pl.ANY)
     smem = pl.BlockSpec(memory_space=pltpu.SMEM)
     vmem = pl.BlockSpec(memory_space=pltpu.VMEM)
     grid_f = (7, planes, 8, 128)
     shapes = [
-        jax.ShapeDtypeStruct(grid_f, F32),
-        jax.ShapeDtypeStruct((3, planes, 8, 128), F32),
-        jax.ShapeDtypeStruct((rows, 32, 128), F32),
-        jax.ShapeDtypeStruct((32, 32), F32),
-        jax.ShapeDtypeStruct((32, 32), F32),
+        pltpu.VMEM(grid_f, F32),
+        pltpu.VMEM((3, planes, 8, 128), F32),
+        pltpu.VMEM((planes // 2, 2, 256, 256), BF16),
+        pltpu.VMEM((32, 32), F32),
+        pltpu.VMEM((32, 32), F32),
     ]
     plane = (planes, 8, 128)
     scratch = [
         pltpu.VMEM(grid_f, F32),
         pltpu.VMEM((3,) + plane, F32),
-        pltpu.VMEM((32 * rows, 128), F32),
+        pltpu.VMEM((32,) + plane, F32),
         pltpu.VMEM(plane, jnp.int32),
         pltpu.VMEM(plane, jnp.int32),
         pltpu.VMEM(plane, F32),
@@ -470,58 +518,52 @@
         pltpu.VMEM((2, planes // 4, 8, 128), F32),
         pltpu.VMEM(plane, F32),
         pltpu.VMEM(plane, F32),
-        pltpu.VMEM((rows, 32, 128), F32),
+        pltpu.VMEM((planes // 2, 768, 256), BF16),
+        pltpu.VMEM((256, 256), F32),
+        pltpu.VMEM((256, 256), F32),
         pltpu.VMEM((4 * GROUP, 8, 128), F32),
         pltpu.SemaphoreType.DMA((5,)),
-        pltpu.SemaphoreType.DMA((3,)),
         pltpu.SemaphoreType.DMA((8,)),
         pltpu.SemaphoreType.DMA((8,)),
-        pltpu.SemaphoreType.DMA((4 * GROUP,)),
-        pltpu.SemaphoreType.DMA((4 * GROUP,)),
+        pltpu.SemaphoreType.DMA((4,)),
+        pltpu.SemaphoreType.DMA((4,)),
     ]
     f, g, y, zt, up = pl.pallas_call(
         kernel,
         out_shape=shapes,
-        in_specs=[any_space] * 5 + [smem] * 2,
-        out_specs=[any_space] * 3 + [vmem] * 2,
+        in_specs=[hbm] * 5 + [smem] * 2,
+        out_specs=[vmem] * 5,
         scratch_shapes=scratch,
         compiler_params=pltpu.CompilerParams(
-            collective_id=0, has_side_effects=True, vmem_limit_bytes=58 << 20
+            collective_id=0, has_side_effects=True, vmem_limit_bytes=54 << 20
         ),
     )(
         split_rows(distributions, grid_f),
         split_rows(gate_states, (3,) + plane),
-        split_rows(history, (32 * rows, 128)),
+        split_rows(history, (32,) + plane),
         split_rows(tissue, plane),
         split_rows(stim_site, plane),
         stim_amp,
         record_column,
     )
-    part = 32
+    parts = 8
     q, f, g, up = pl.pallas_call(
         basis_kernel,
-        grid=(rows // part,),
         out_shape=[
-            jax.ShapeDtypeStruct((32, rows, 128), F32),
-            jax.ShapeDtypeStruct((7, rows, 128), F32),
-            jax.ShapeDtypeStruct((3, rows, 128), F32),
+            jax.ShapeDtypeStruct((32,) + plane, F32),
+            jax.ShapeDtypeStruct(grid_f, F32),
+            jax.ShapeDtypeStruct((3,) + plane, F32),
             jax.ShapeDtypeStruct((32, 32), F32),
         ],
-        in_specs=[
-            pl.BlockSpec((part, 32, 128), lambda i: (i, 0, 0)),
-            pl.BlockSpec((7, part, 128), lambda i: (0, i, 0)),
-            pl.BlockSpec((3, part, 128), lambda i: (0, i, 0)),
-            pl.BlockSpec((32, 32), lambda i: (0, 0)),
-            pl.BlockSpec((32, 32), lambda i: (0, 0)),
+        in_specs=[vmem] * 5,
+        out_specs=[any_space] * 4,
+        scratch_shapes=[
+            pltpu.VMEM((32,) + plane, F32),
+            pltpu.SemaphoreType.DMA((parts,)),
+            pltpu.SemaphoreType.DMA((3,)),
         ],
-        out_specs=[
-            pl.BlockSpec((32, part, 128), lambda i: (0, i, 0)),
-            pl.BlockSpec((7, part, 128), lambda i: (0, i, 0)),
-            pl.BlockSpec((3, part, 128), lambda i: (0, i, 0)),
-            pl.BlockSpec((32, 32), lambda i: (0, 0)),
-        ],
-        compiler_params=pltpu.CompilerParams(vmem_limit_bytes=58 << 20),
-    )(y, f.reshape(7, rows, 128), g.reshape(3, rows, 128), zt, up)
+        compiler_params=pltpu.CompilerParams(vmem_limit_bytes=48 << 20),
+    )(y, f, g, zt, up)
     return (
         join_rows(f, distributions.shape),
         join_rows(g, gate_states.shape),

time: 69.3 us -> 45.9 us (0.66)
  Pallas kernels: 68.4 us -> 45.2 us
    pallas_call x2, Pallas kernels: 68.4 us -> 45.2 us  [the longest x1 42.3 us: local(): pl.pallas_call(kernel, out_shape=shapes, in_specs=[hbm] * 5 + [smem] * 2,...]
where the time goes in v1:
time: 45.9 us; the launch traced here: 45.8 us
  Pallas kernels  45.2 us (98%)
  between operations  0.64 us (1%)
    pallas_call x1, Pallas kernels, local(): pl.pallas_call(kernel, out_shape=shapes, in_specs=[hbm] * 5 + [smem] * 2,...  42.3 us
    pallas_call x1, Pallas kernels, local(): pl.pallas_call(basis_kernel, out_shape=[jax.ShapeDtypeStruct((32,) + plan...  2.91 us

profile of v1, /device:TPU:1, one launch (start us, length us, event | category | flops | bytes accessed | tf_op | source)
XLA Modules:
  0.0 45.8 jit_solution(17117688898220229724)
XLA Ops:
  0.6 42.3 %shard_map.102 = (f32[7,32,8,128]{3,2,1,0:T(8,128)S(1)}, f32[3,32,8,128]{3,2,1,0:T(8,128)S(1)}, bf16[16,2,256,256]{3,2,1,0:T(8,128)(2,1)S(1)}, f32[32,32]{1,0:T(8,128)S(1)}, f32[32,32]{1,0:T(8,128)S(1)}) custom-call(f32[7,32,8,128]{3,2,1,0:T(8,128)} %bitcast.41, f32[3,32,8,128]{3,2,1,0:T(8,128)} %bitcast.42, f32[32,32,8,128]{3,2,1,0:T(8,128)} %bitcast.40, ...), custom_call_target="tpu_custom_call" | custom-call | tf_op jit(solution)/shard_map/pallas_call | solution.py:531
  42.9 2.9 %shard_map.103 = (f32[32,32,8,128]{3,2,1,0:T(8,128)}, f32[7,32,8,128]{3,2,1,0:T(8,128)}, f32[3,32,8,128]{3,2,1,0:T(8,128)}, f32[32,32]{1,0:T(8,128)}) custom-call(bf16[16,2,256,256]{3,2,1,0:T(8,128)(2,1)S(1)} %get-tuple-element.13.y_ref, f32[7,32,8,128]{3,2,1,0:T(8,128)S(1)} %get-tuple-element.14.f_ref, f32[3,32,8,128]{3,2,1,0:T(8,128)S(1)} %get-tuple-element.15.g_ref, ...), custom_call_target="tpu_custom_call" | custom-call | tf_op jit(solution)/shard_map/pallas_call | solution.py:550

commit v2 on v1

--- a/solution.py
+++ b/solution.py
@@ -16,7 +16,8 @@
 BF16 = jnp.bfloat16
 NT = (((1,), (1,)), ((), ()))
 GROUP = 16
-PANEL = 4
+PANEL = 16
+STEP = 8
 
 
 def split_rows(a, shape):
@@ -107,7 +108,7 @@
     f_hbm, g_hbm, x_hbm, t_hbm, s_hbm, amp, rc,
     f_out, g_out, y_out, zt_ref, up_ref,
     fv, gv, xv, tv, sv, stim, cc, cxp, cxm, ysp, ysm, yrp, yrm, u1, u2,
-    xs, acc1, acc2, red,
+    xs, red,
     load_sem, hs_sem, hr_sem, as_sem, ar_sem,
 ):
     planes = fv.shape[1]
@@ -314,18 +315,15 @@
     def pair(x):
         return jnp.concatenate([xv[:, 2 * x].reshape(256, 128), xv[:, 2 * x + 1].reshape(256, 128)], axis=1)
 
-    acc1[...] = jnp.zeros((256, 256), F32)
-
-    def old_gram(i, carry):
-        parts = [pair(2 * i + k).astype(BF16) for k in range(2)]
-        for k in range(2):
-            xs[2 * i + k, :256] = parts[k]
+    def old_gram(i, acc):
+        parts = [pair(STEP * i + k).astype(BF16) for k in range(STEP)]
+        for k in range(STEP):
+            xs[STEP * i + k, :256] = parts[k]
         hi = jnp.concatenate(parts, axis=1)
-        acc1[...] += lax.dot_general(hi, hi, NT, preferred_element_type=F32)
-        return carry
-
-    lax.fori_loop(0, quads, old_gram, 0)
-    block = packed(folded(acc1[...]))
+        return acc + lax.dot_general(hi, hi, NT, preferred_element_type=F32)
+
+    acc = lax.fori_loop(0, planes // 2 // STEP, old_gram, jnp.zeros((256, 256), F32))
+    block = packed(folded(acc))
     pl.semaphore_wait(barrier, 4 + 2 * (GROUP - 1))
     reduce_send(0, 0, block)
 
@@ -375,7 +373,7 @@
     gram = jnp.where(taken, eye, gram * (1.0 + eye * 2.0**-16))
     _, inv0, pivot = eliminate(gram)
     t0 = (inv0 * (1.0 / jnp.sqrt(pivot))).astype(BF16)
-    spread = spread_rows(t0)
+    spread = spread_rows(t0, True, False)
     spread = jnp.concatenate([spread, spread, spread], axis=1)
 
     settle_halos(1)
@@ -390,40 +388,33 @@
 
     lax.fori_loop(0, quads, fourth, 0)
 
-    column = lax.broadcasted_iota(jnp.int32, (32, 8, 256), 0)
+    column = lax.broadcasted_iota(jnp.int32, (32, 256), 0)
     is1, is2 = column == rc[0], column == rc[1]
-    acc1[...] = jnp.zeros((256, 256), F32)
-    acc2[...] = jnp.zeros((256, 256), F32)
-
-    def whitened(i):
-        y = jnp.dot(spread, xs[i], preferred_element_type=F32)
-        new1 = jnp.concatenate([u1[2 * i], u1[2 * i + 1]], axis=1)
-        new2 = jnp.concatenate([u2[2 * i], u2[2 * i + 1]], axis=1)
-        y = jnp.where(is1, new1[None], jnp.where(is2, new2[None], y.reshape(32, 8, 256)))
-        y = y.reshape(256, 256)
-        hi = y.astype(BF16)
-        lo = (y - hi.astype(F32)).astype(BF16)
-        y_out[i, 0] = hi
-        y_out[i, 1] = lo
-        return hi, lo
-
-    def new_gram(i, carry):
-        (h1, l1), (h2, l2) = whitened(2 * i), whitened(2 * i + 1)
-        every = jnp.concatenate([h1, h2, l1, l2], axis=1)
-        acc1[...] += lax.dot_general(every, every, NT, preferred_element_type=F32)
-        acc2[...] += lax.dot_general(
-            every[:, :512], every[:, 512:], NT, preferred_element_type=F32
-        )
-        return carry
-
-    lax.fori_loop(0, quads, new_gram, 0)
-    cross = folded(acc2[...])
-    gram = folded(acc1[...]) + (
-        cross
-        + lax.dot_general(
-            eye, cross, NT, precision=lax.Precision.HIGHEST, preferred_element_type=F32
-        )
-    )
+
+    def new_gram(i, acc):
+        his, los = [], []
+        for k in range(STEP):
+            at = STEP * i + k
+            y = jnp.dot(spread, xs[at], preferred_element_type=F32)
+            new1 = jnp.concatenate([u1[2 * at], u1[2 * at + 1]], axis=1)
+            new2 = jnp.concatenate([u2[2 * at], u2[2 * at + 1]], axis=1)
+            for r in range(8):
+                part = y[32 * r : 32 * r + 32]
+                part = jnp.where(is2, new2[r : r + 1], part)
+                part = jnp.where(is1, new1[r : r + 1], part)
+                hi = part.astype(BF16)
+                lo = (part - hi.astype(F32)).astype(BF16)
+                y_out[at, 0, 32 * r : 32 * r + 32] = hi
+                y_out[at, 1, 32 * r : 32 * r + 32] = lo
+                his.append(hi)
+                los.append(lo)
+        both = jnp.concatenate(
+            [jnp.concatenate(his, axis=1), jnp.concatenate(los, axis=1)], axis=0
+        )
+        return acc + lax.dot_general(both, both, NT, preferred_element_type=F32)
+
+    acc = lax.fori_loop(0, planes // 2 // STEP, new_gram, jnp.zeros((64, 64), F32))
+    gram = acc[:32, :32] + ((acc[:32, 32:] + acc[32:, :32]) + acc[32:, 32:])
     reduce_send(1, 0, packed(gram))
     _, inv0, pivot = eliminate(t0.astype(F32))
     back = inv0 * (1.0 / pivot)
@@ -444,14 +435,21 @@
             reduce_all(which, stage).wait_send()
 
 
-def spread_rows(t):
-    place = lax.broadcasted_iota(jnp.int32, (256, 32), 0) // 8
-    pick = jnp.where(place == lax.broadcasted_iota(jnp.int32, (256, 32), 1), 1.0, 0.0).astype(BF16)
-    half = jnp.dot(pick, t, preferred_element_type=F32).astype(BF16)
-    full = lax.dot_general(half, pick, NT, preferred_element_type=F32)
-    row = lax.rem(lax.broadcasted_iota(jnp.int32, (256, 256), 0), 8)
-    col = lax.rem(lax.broadcasted_iota(jnp.int32, (256, 256), 1), 8)
-    return jnp.where(row == col, full, 0.0).astype(BF16)
+def places(shape, dim, row_first):
+    at = lax.broadcasted_iota(jnp.int32, shape, dim)
+    return (at // 32, lax.rem(at, 32)) if row_first else (lax.rem(at, 8), at // 8)
+
+
+def spread_rows(t, out_row_first, in_row_first):
+    index = lax.broadcasted_iota(jnp.int32, (256, 32), 1)
+
+    def pick(row_first):
+        return jnp.where(places((256, 32), 0, row_first)[1] == index, 1.0, 0.0).astype(BF16)
+
+    half = jnp.dot(pick(out_row_first), t, preferred_element_type=F32).astype(BF16)
+    full = lax.dot_general(half, pick(in_row_first), NT, preferred_element_type=F32)
+    same = places((256, 256), 0, out_row_first)[0] == places((256, 256), 1, in_row_first)[0]
+    return jnp.where(same, full, 0.0).astype(BF16)
 
 
 def basis_kernel(
@@ -467,8 +465,8 @@
         copy.start()
     z = z_ref[...]
     hi = z.astype(BF16)
-    spread = spread_rows(hi)
-    rest = spread_rows((z - hi.astype(F32)).astype(BF16))
+    spread = spread_rows(hi, False, True)
+    rest = spread_rows((z - hi.astype(F32)).astype(BF16), False, True)
     wide = jnp.concatenate([spread, spread, rest], axis=1)
     stores = []
     for i in range(parts):
@@ -519,8 +517,6 @@
         pltpu.VMEM(plane, F32),
         pltpu.VMEM(plane, F32),
         pltpu.VMEM((planes // 2, 768, 256), BF16),
-        pltpu.VMEM((256, 256), F32),
-        pltpu.VMEM((256, 256), F32),
         pltpu.VMEM((4 * GROUP, 8, 128), F32),
         pltpu.SemaphoreType.DMA((5,)),
         pltpu.SemaphoreType.DMA((8,)),

time: 45.9 us -> 41.1 us (0.90)
  Pallas kernels: 45.2 us -> 40.3 us
    pallas_call x1, Pallas kernels: 42.3 us -> 37.4 us  [local(): pl.pallas_call(kernel, out_shape=shapes, in_specs=[hbm] * 5 + [smem] * 2,...]
where the time goes in v2:
time: 41.1 us; the launch traced here: 41 us
  Pallas kernels  40.3 us (98%)
  between operations  0.64 us (2%)
    pallas_call x1, Pallas kernels, local(): pl.pallas_call(kernel, out_shape=shapes, in_specs=[hbm] * 5 + [smem] * 2,...  37.4 us
    pallas_call x1, Pallas kernels, local(): pl.pallas_call(basis_kernel, out_shape=[jax.ShapeDtypeStruct((32,) + plan...  2.9 us

profile of v2, /device:TPU:1, one launch (start us, length us, event | category | flops | bytes accessed | tf_op | source)
XLA Modules:
  0.0 41.0 jit_solution(3250752226141378220)
XLA Ops:
  0.6 37.4 %shard_map.102 = (f32[7,32,8,128]{3,2,1,0:T(8,128)S(1)}, f32[3,32,8,128]{3,2,1,0:T(8,128)S(1)}, bf16[16,2,256,256]{3,2,1,0:T(8,128)(2,1)S(1)}, f32[32,32]{1,0:T(8,128)S(1)}, f32[32,32]{1,0:T(8,128)S(1)}) custom-call(f32[7,32,8,128]{3,2,1,0:T(8,128)} %bitcast.41, f32[3,32,8,128]{3,2,1,0:T(8,128)} %bitcast.42, f32[32,32,8,128]{3,2,1,0:T(8,128)} %bitcast.40, ...), custom_call_target="tpu_custom_call" | custom-call | tf_op jit(solution)/shard_map/pallas_call | solution.py:527
  38.1 2.9 %shard_map.103 = (f32[32,32,8,128]{3,2,1,0:T(8,128)}, f32[7,32,8,128]{3,2,1,0:T(8,128)}, f32[3,32,8,128]{3,2,1,0:T(8,128)}, f32[32,32]{1,0:T(8,128)}) custom-call(bf16[16,2,256,256]{3,2,1,0:T(8,128)(2,1)S(1)} %get-tuple-element.13.y_ref, f32[7,32,8,128]{3,2,1,0:T(8,128)S(1)} %get-tuple-element.14.f_ref, f32[3,32,8,128]{3,2,1,0:T(8,128)S(1)} %get-tuple-element.15.g_ref, ...), custom_call_target="tpu_custom_call" | custom-call | tf_op jit(solution)/shard_map/pallas_call | solution.py:546

commit v3 on v2

--- a/solution.py
+++ b/solution.py
@@ -105,10 +105,10 @@
 
 
 def kernel(
-    f_hbm, g_hbm, x_hbm, t_hbm, s_hbm, amp, rc,
-    f_out, g_out, y_out, zt_ref, up_ref,
+    f_hbm, g_hbm, x_hbm, t_hbm, s_hbm, amp_hbm, rc_hbm,
+    f_out, g_out, y_out, zt_ref, r2_ref, back_ref,
     fv, gv, xv, tv, sv, stim, cc, cxp, cxm, ysp, ysm, yrp, yrm, u1, u2,
-    xs, red,
+    xs, red, amp, rc,
     load_sem, hs_sem, hr_sem, as_sem, ar_sem,
 ):
     planes = fv.shape[1]
@@ -117,10 +117,12 @@
     slab, tile = lax.axis_index("slab"), lax.axis_index("tile")
     core, yy, zz = lax.rem(tile, 2), lax.rem(tile // 2, 4), tile // 8
 
+    halves = [pl.ds(i * (planes // 2), planes // 2) for i in range(2)]
     loads = [
         pltpu.make_async_copy(src, dst, load_sem.at[i])
         for i, (src, dst) in enumerate(
-            ((x_hbm, xv), (f_hbm, fv), (t_hbm, tv), (s_hbm, sv), (g_hbm, gv))
+            [(x_hbm.at[:, half], xv.at[:, half]) for half in halves]
+            + [(f_hbm, fv), (t_hbm, tv), (s_hbm, sv), (g_hbm, gv), (amp_hbm, amp), (rc_hbm, rc)]
         )
     ]
     for copy in loads:
@@ -310,7 +312,6 @@
         pick = jnp.where(place == lax.broadcasted_iota(jnp.int32, (256, 32), 1), 1.0, 0.0)
         return jnp.dot(m, pick, precision=lax.Precision.HIGHEST, preferred_element_type=F32)
 
-    loads[0].wait()
 
     def pair(x):
         return jnp.concatenate([xv[:, 2 * x].reshape(256, 128), xv[:, 2 * x + 1].reshape(256, 128)], axis=1)
@@ -322,12 +323,16 @@
         hi = jnp.concatenate(parts, axis=1)
         return acc + lax.dot_general(hi, hi, NT, preferred_element_type=F32)
 
-    acc = lax.fori_loop(0, planes // 2 // STEP, old_gram, jnp.zeros((256, 256), F32))
+    share = planes // 4 // STEP
+    acc = jnp.zeros((256, 256), F32)
+    for half in range(2):
+        loads[half].wait()
+        acc = lax.fori_loop(half * share, (half + 1) * share, old_gram, acc)
     block = packed(folded(acc))
     pl.semaphore_wait(barrier, 4 + 2 * (GROUP - 1))
     reduce_send(0, 0, block)
 
-    for copy in loads[1:]:
+    for copy in loads[2:]:
         copy.wait()
 
     def first(q, carry):
@@ -368,6 +373,18 @@
     for copy in halos(1):
         copy.start()
 
+    settle_halos(1)
+
+    def fourth(q, carry):
+        p = pl.ds(q * 4, 4)
+        f, u = propagate(1, q, tv[p])
+        u2[p] = u
+        for i in range(7):
+            f_out[i, p] = f[i]
+        return carry
+
+    lax.fori_loop(0, quads, fourth, 0)
+
     gram = unpacked(reduce_sum(0, 1))
     taken = (ri == rc[0]) | (ri == rc[1]) | (ci == rc[0]) | (ci == rc[1])
     gram = jnp.where(taken, eye, gram * (1.0 + eye * 2.0**-16))
@@ -375,18 +392,6 @@
     t0 = (inv0 * (1.0 / jnp.sqrt(pivot))).astype(BF16)
     spread = spread_rows(t0, True, False)
     spread = jnp.concatenate([spread, spread, spread], axis=1)
-
-    settle_halos(1)
-
-    def fourth(q, carry):
-        p = pl.ds(q * 4, 4)
-        f, u = propagate(1, q, tv[p])
-        u2[p] = u
-        for i in range(7):
-            f_out[i, p] = f[i]
-        return carry
-
-    lax.fori_loop(0, quads, fourth, 0)
 
     column = lax.broadcasted_iota(jnp.int32, (32, 256), 0)
     is1, is2 = column == rc[0], column == rc[1]
@@ -417,15 +422,13 @@
     gram = acc[:32, :32] + ((acc[:32, 32:] + acc[32:, :32]) + acc[32:, 32:])
     reduce_send(1, 0, packed(gram))
     _, inv0, pivot = eliminate(t0.astype(F32))
-    back = inv0 * (1.0 / pivot)
+    back_ref[...] = inv0 * (1.0 / pivot)
     reduce_send(1, 1, reduce_sum(1, 0))
     r2, inv2, pivot = eliminate(unpacked(reduce_sum(1, 1)))
     scale = 1.0 / jnp.sqrt(pivot)
     norm = math.sqrt(planes * 1024 * slabs * tiles)
     zt_ref[...] = inv2 * (scale * norm)
-    up_ref[...] = lax.dot_general(
-        r2 * scale, back, NT, precision=lax.Precision.HIGHEST, preferred_element_type=F32
-    ) * (1.0 / norm)
+    r2_ref[...] = r2 * (scale * (1.0 / norm))
 
     for step in range(2):
         for copy in halos(step):
@@ -453,15 +456,16 @@
 
 
 def basis_kernel(
-    y_ref, f_ref, g_ref, z_ref, r_ref, q_hbm, f_hbm, g_hbm, r_hbm, qv, q_sem, p_sem
+    y_ref, f_ref, g_ref, z_ref, r2_ref, back_ref,
+    q_hbm, f_hbm, g_hbm, up_hbm, qv, up, q_sem, p_sem,
 ):
     parts = q_sem.shape[0]
     pairs = y_ref.shape[0] // parts
     passed = [
         pltpu.make_async_copy(src, dst, p_sem.at[i])
-        for i, (src, dst) in enumerate(((f_ref, f_hbm), (g_ref, g_hbm), (r_ref, r_hbm)))
+        for i, (src, dst) in enumerate(((f_ref, f_hbm), (g_ref, g_hbm), (up, up_hbm)))
     ]
-    for copy in passed:
+    for copy in passed[:2]:
         copy.start()
     z = z_ref[...]
     hi = z.astype(BF16)
@@ -481,6 +485,15 @@
             pltpu.make_async_copy(qv.at[:, planes], q_hbm.at[:, planes], q_sem.at[i])
         )
         stores[-1].start()
+        if i == parts // 2:
+            up[...] = lax.dot_general(
+                r2_ref[...],
+                back_ref[...],
+                NT,
+                precision=lax.Precision.HIGHEST,
+                preferred_element_type=F32,
+            )
+            passed[2].start()
     for copy in passed + stores:
         copy.wait()
 
@@ -489,13 +502,13 @@
     planes = distributions.shape[1]
     hbm = pl.BlockSpec(memory_space=pltpu.HBM)
     any_space = pl.BlockSpec(memory_space=pl.ANY)
-    smem = pl.BlockSpec(memory_space=pltpu.SMEM)
     vmem = pl.BlockSpec(memory_space=pltpu.VMEM)
     grid_f = (7, planes, 8, 128)
     shapes = [
         pltpu.VMEM(grid_f, F32),
         pltpu.VMEM((3, planes, 8, 128), F32),
         pltpu.VMEM((planes // 2, 2, 256, 256), BF16),
+        pltpu.VMEM((32, 32), F32),
         pltpu.VMEM((32, 32), F32),
         pltpu.VMEM((32, 32), F32),
     ]
@@ -518,17 +531,19 @@
         pltpu.VMEM(plane, F32),
         pltpu.VMEM((planes // 2, 768, 256), BF16),
         pltpu.VMEM((4 * GROUP, 8, 128), F32),
-        pltpu.SemaphoreType.DMA((5,)),
+        pltpu.SMEM((8,), F32),
+        pltpu.SMEM((2,), jnp.int32),
+        pltpu.SemaphoreType.DMA((8,)),
         pltpu.SemaphoreType.DMA((8,)),
         pltpu.SemaphoreType.DMA((8,)),
         pltpu.SemaphoreType.DMA((4,)),
         pltpu.SemaphoreType.DMA((4,)),
     ]
-    f, g, y, zt, up = pl.pallas_call(
+    f, g, y, zt, r2, back = pl.pallas_call(
         kernel,
         out_shape=shapes,
-        in_specs=[hbm] * 5 + [smem] * 2,
-        out_specs=[vmem] * 5,
+        in_specs=[hbm] * 7,
+        out_specs=[vmem] * 6,
         scratch_shapes=scratch,
         compiler_params=pltpu.CompilerParams(
             collective_id=0, has_side_effects=True, vmem_limit_bytes=54 << 20
@@ -551,15 +566,16 @@
             jax.ShapeDtypeStruct((3,) + plane, F32),
             jax.ShapeDtypeStruct((32, 32), F32),
         ],
-        in_specs=[vmem] * 5,
+        in_specs=[vmem] * 6,
         out_specs=[any_space] * 4,
         scratch_shapes=[
             pltpu.VMEM((32,) + plane, F32),
+            pltpu.VMEM((32, 32), F32),
             pltpu.SemaphoreType.DMA((parts,)),
             pltpu.SemaphoreType.DMA((3,)),
         ],
         compiler_params=pltpu.CompilerParams(vmem_limit_bytes=48 << 20),
-    )(y, f, g, zt, up)
+    )(y, f, g, zt, r2, back)
     return (
         join_rows(f, distributions.shape),
         join_rows(g, gate_states.shape),

time: 41.1 us -> 40.7 us (level)
    pallas_call x1, Pallas kernels: 37.4 us -> 36.9 us  [local(): pl.pallas_call(kernel, out_shape=shapes, in_specs=[hbm] * 7, out_specs=[v...]
where the time goes in v3:
time: 40.7 us; the launch traced here: 40.6 us
  Pallas kernels  39.9 us (98%)
  between operations  0.64 us (2%)
    pallas_call x1, Pallas kernels, local(): pl.pallas_call(kernel, out_shape=shapes, in_specs=[hbm] * 7, out_specs=[v...  36.9 us
    pallas_call x1, Pallas kernels, local(): pl.pallas_call(basis_kernel, out_shape=[jax.ShapeDtypeStruct((32,) + plan...  3.05 us

profile of v3, /device:TPU:1, one launch (start us, length us, event | category | flops | bytes accessed | tf_op | source)
XLA Modules:
  0.0 40.6 jit_solution(9954611634556016243)
XLA Ops:
  0.6 36.9 %shard_map.102 = (f32[7,32,8,128]{3,2,1,0:T(8,128)S(1)}, f32[3,32,8,128]{3,2,1,0:T(8,128)S(1)}, bf16[16,2,256,256]{3,2,1,0:T(8,128)(2,1)S(1)}, f32[32,32]{1,0:T(...) custom-call(f32[7,32,8,128]{3,2,1,0:T(8,128)} %bitcast.41, f32[3,32,8,128]{3,2,1,0:T(8,128)} %bitcast.42, ...), custom_call_target="tpu_custom_call" | custom-call | tf_op jit(solution)/shard_map/pallas_call | solution.py:542
  37.5 3.0 %shard_map.103 = (f32[32,32,8,128]{3,2,1,0:T(8,128)}, f32[7,32,8,128]{3,2,1,0:T(8,128)}, f32[3,32,8,128]{3,2,1,0:T(8,128)}, f32[32,32]{1,0:T(8,128)}) custom-call(bf16[16,2,256,256]{3,2,1,0:T(8,128)(2,1)S(1)} %get-tuple-element.14.y_ref, f32[7,32,8,128]{3,2,1,0:T(8,128)S(1)} %get-tuple-element.15.f_ref, f32[3,32,8,128]{3,2,1,0:T(8,128)S(1)} %get-tuple-element.16.g_ref, ...), custom_call_target="tpu_custom_call" | custom-call | tf_op jit(solution)/shard_map/pallas_call | solution.py:561

commit v4 on v3

--- a/solution.py
+++ b/solution.py
@@ -144,12 +144,8 @@
     for dev in (right, left, up, down):
         pl.semaphore_signal(barrier, inc=1, device_id=dev, device_id_type=MESH)
     for stage in range(2):
-
-        def greet(k, carry, stage=stage):
+        for k in range(1, GROUP):
             pl.semaphore_signal(barrier, inc=1, device_id=partner(stage, k), device_id_type=MESH)
-            return carry
-
-        lax.fori_loop(1, GROUP, greet, 0)
 
     row4 = lax.broadcasted_iota(jnp.int32, (8, 128), 0)
     lane = lax.broadcasted_iota(jnp.int32, (4, 8, 128), 2)

time: 40.7 us -> 40.6 us (level)
  no operation moved by 1% of the time
where the time goes in v4:
time: 40.6 us; the launch traced here: 40.5 us
  Pallas kernels  39.9 us (98%)
  between operations  0.64 us (2%)
    pallas_call x1, Pallas kernels, local(): pl.pallas_call(kernel, out_shape=shapes, in_specs=[hbm] * 7, out_specs=[v...  36.8 us
    pallas_call x1, Pallas kernels, local(): pl.pallas_call(basis_kernel, out_shape=[jax.ShapeDtypeStruct((32,) + plan...  3.05 us

profile of v4, /device:TPU:1, one launch (start us, length us, event | category | flops | bytes accessed | tf_op | source)
XLA Modules:
  0.0 40.5 jit_solution(7941501869735095821)
XLA Ops:
  0.6 36.8 %shard_map.102 = (f32[7,32,8,128]{3,2,1,0:T(8,128)S(1)}, f32[3,32,8,128]{3,2,1,0:T(8,128)S(1)}, bf16[16,2,256,256]{3,2,1,0:T(8,128)(2,1)S(1)}, f32[32,32]{1,0:T(...) custom-call(f32[7,32,8,128]{3,2,1,0:T(8,128)} %bitcast.41, f32[3,32,8,128]{3,2,1,0:T(8,128)} %bitcast.42, ...), custom_call_target="tpu_custom_call" | custom-call | tf_op jit(solution)/shard_map/pallas_call | solution.py:538
  37.5 3.0 %shard_map.103 = (f32[32,32,8,128]{3,2,1,0:T(8,128)}, f32[7,32,8,128]{3,2,1,0:T(8,128)}, f32[3,32,8,128]{3,2,1,0:T(8,128)}, f32[32,32]{1,0:T(8,128)}) custom-call(bf16[16,2,256,256]{3,2,1,0:T(8,128)(2,1)S(1)} %get-tuple-element.14.y_ref, f32[7,32,8,128]{3,2,1,0:T(8,128)S(1)} %get-tuple-element.15.f_ref, f32[3,32,8,128]{3,2,1,0:T(8,128)S(1)} %get-tuple-element.16.g_ref, ...), custom_call_target="tpu_custom_call" | custom-call | tf_op jit(solution)/shard_map/pallas_call | solution.py:557
